TPU v7x, 32 devices: a whole 2x2x4 slice. The times are simulated.
32 devices in a mesh: groups: 2 (over y), seq: 4 (over z), tensor: 4 (over x, core).
Axes of the slice: x: 2, y: 2, z: 4, core: 2. Of those that a mesh axis runs over, the one named last changes fastest.
Arguments:
- queries: bfloat16 [2048, 3072], P(('groups', 'seq'), 'tensor'), parts along dimension 0, may hold values from -8 to 8
- keys: bfloat16 [2048, 3072], P(('groups', 'seq'), 'tensor'), parts along dimension 0, may hold values from -6 to 6
- values: bfloat16 [2048, 3072], P(('groups', 'seq'), 'tensor'), parts along dimension 0, may hold values from -110 to 110
- text_keys: bfloat16 [128, 3072], P(('groups', 'seq'), 'tensor'), parts along dimension 0, may hold values from -9 to 9
- text_values: bfloat16 [128, 3072], P(('groups', 'seq'), 'tensor'), parts along dimension 0, may hold values from -24 to 24
- text_len: int32 [2], P('groups'), parts along dimension 0, may hold values from 1 to 64
- uncond: bfloat16 [2048, 3072], P(('groups', 'seq'), 'tensor'), parts along dimension 0, may hold values from -10 to 10
- flags: int32 [2048], P(('groups', 'seq')), parts along dimension 0, may hold values 0 or 1
- guide_num: int32 [2], P('groups'), parts along dimension 0, may hold values from 768 to 2559
- guide_den: int32 [2], P('groups'), parts along dimension 0, may hold values from 512 to 1087
Outputs:
- guided: bfloat16 [2048, 3072], P(('groups', 'seq'), 'tensor'), parts along dimension 0
There are 2 independent parts, one for each index of `groups`. A program takes and returns all parts, laid end to end along the dimension named above; each array names one. Nothing has to cross between parts.
All inputs are finite; a program needn't handle non-finite values. No bound on the sum of `flags` on one device may be relied on, other than what follows from the above.
Results may differ from a plain program's by a relative error of at most 0.0045.
Values may be sent and summed in bfloat16 or wider, within the bound.
A program may use at most 64 MiB of HBM per device.

v0:
```python
import math

import jax
import jax.numpy as jnp
from jax import lax
from jax.sharding import PartitionSpec as P

HEAD_DIM = 128


def local(
    queries, keys, values, text_keys, text_values, text_len, uncond, flags, guide_num, guide_den
):
    tok_rows, width = queries.shape
    heads = width // HEAD_DIM
    factor = 1.0 / math.sqrt(HEAD_DIM)
    limit = text_len[0]

    def attend(state, query_heads, key_piece, value_piece, live):
        rows = key_piece.shape[0]
        key_heads = key_piece.reshape(rows, heads, HEAD_DIM)
        value_heads = value_piece.reshape(rows, heads, HEAD_DIM)
        scores = (
            jnp.einsum("qhd,khd->hqk", query_heads, key_heads, preferred_element_type=jnp.float32)
            * factor
        )
        if live is not None:
            scores = jnp.where(live[None, None, :], scores, -1e30)
        top, total, accum = state
        new_top = jnp.maximum(top, jnp.max(scores, axis=2))
        fade = jnp.exp(top - new_top)
        weights = jnp.exp(scores - new_top[:, :, None])
        total = total * fade + jnp.sum(weights, axis=2)
        mixed = jnp.einsum(
            "hqk,khd->hqd",
            weights.astype(jnp.bfloat16),
            value_heads,
            preferred_element_type=jnp.float32,
        )
        accum = accum * fade[:, :, None] + mixed
        return (new_top, total, accum)

    def blocked(state, query_heads, key_piece, value_piece, block):
        rows = key_piece.shape[0]
        if rows <= block or rows % block != 0:
            return attend(state, query_heads, key_piece, value_piece, None)
        key_blocks = key_piece.reshape(rows // block, block, width)
        value_blocks = value_piece.reshape(rows // block, block, width)

        def step_block(carry, pair):
            return (attend(carry, query_heads, pair[0], pair[1], None), None)

        return lax.scan(step_block, state, (key_blocks, value_blocks))[0]

    query_heads = queries.reshape(tok_rows, heads, HEAD_DIM)
    state = blocked(
        (
            jnp.full((heads, tok_rows), -1e30, jnp.float32),
            jnp.zeros((heads, tok_rows), jnp.float32),
            jnp.zeros((heads, tok_rows, HEAD_DIM), jnp.float32),
        ),
        query_heads,
        lax.all_gather(keys, "seq", axis=0, tiled=True),
        lax.all_gather(values, "seq", axis=0, tiled=True),
        1024,
    )
    all_text_keys, all_text_values = (
        lax.all_gather(text_keys, "seq", axis=0, tiled=True),
        lax.all_gather(text_values, "seq", axis=0, tiled=True),
    )
    text_live = jnp.arange(all_text_keys.shape[0]) < limit
    state = attend(state, query_heads, all_text_keys, all_text_values, text_live)
    top, total, accum = state
    cond = (accum / total[:, :, None]).transpose(1, 0, 2).reshape(tok_rows, width)
    diff = cond - uncond.astype(jnp.float32)
    inner, square = lax.psum((jnp.sum(diff * cond, axis=1), jnp.sum(cond * cond, axis=1)), "tensor")
    full_width = width * lax.axis_size("tensor")
    coef = inner / full_width / (square / full_width + 1e-06)
    scale = guide_num[0].astype(jnp.float32) / guide_den[0].astype(jnp.float32)
    steered = cond + (scale - 1.0) * (diff - coef[:, None] * cond)
    return jnp.where(flags[:, None] > 0, steered, cond).astype(jnp.bfloat16)


def solution(mesh):
    return jax.shard_map(
        local,
        mesh=mesh,
        in_specs=(
            P(("groups", "seq"), "tensor"),
            P(("groups", "seq"), "tensor"),
            P(("groups", "seq"), "tensor"),
            P(("groups", "seq"), "tensor"),
            P(("groups", "seq"), "tensor"),
            P("groups"),
            P(("groups", "seq"), "tensor"),
            P(("groups", "seq")),
            P("groups"),
            P("groups"),
        ),
        out_specs=P(("groups", "seq"), "tensor"),
        check_vma=False,
    )
```

profile of v0, /device:TPU:0, one launch (start us, length us, event | category | flops | bytes accessed | tf_op | source)
XLA Modules:
  0.0 109.8 jit_solution(13318879677277679962)
XLA Ops:
  6.5 0.0 all-gather.3.cloned.1.call-start
  6.5 1.9 %copy.20 = bf16[256,768]{0,1:T(8,128)(2,1)} copy(bf16[256,768]{1,0:T(8,128)(2,1)} %param.11) | data formatting | bytes 786432 | tf_op args[1]
  8.5 0.0 all-gather.3.cloned.1.call-update
  8.5 0.0 all-gather.5.cloned.1.call-start
  8.5 0.7 all-gather.5.cloned.1.call-update
  9.2 1.2 %copy.19 = bf16[256,768]{0,1:T(8,128)(2,1)S(1)} copy(bf16[256,768]{1,0:T(8,128)(2,1)} %param.10) | data formatting | bytes 786432 | tf_op args[0]
  12.4 15.7 %all_gather.14 = bf16[64,768]{1,0:T(8,128)(2,1)S(1)} all-gather(bf16[16,768]{1,0:T(8,128)(2,1)} %param.13), channel_id=1, replica_groups=mesh['groups'=2,'seq'=4,'tensor'=4] {'seq'}, dimensions={0}, use_global_device_ids=true | all-gather | bytes 122880 | tf_op jit(solution)/shard_map/all_gather | solution.py:68
  28.0 17.1 %all_gather.15 = bf16[64,768]{1,0:T(8,128)(2,1)S(1)} all-gather(bf16[16,768]{1,0:T(8,128)(2,1)} %param.14), channel_id=1, replica_groups=mesh['groups'=2,'seq'=4,'tensor'=4] {'seq'}, dimensions={0}, use_global_device_ids=true | all-gather | bytes 122880 | tf_op jit(solution)/shard_map/all_gather | solution.py:69
  45.2 0.7 broadcast_compare_fusion
  45.9 0.2 fusion.34
  46.1 5.7 %all-gather.3.cloned.1.call-done = bf16[1024,768]{0,1:T(8,128)(2,1)} async-done(((bf16[256,768]{0,1:T(8,128)(2,1)}), bf16[1024,768]{0,1:T(8,128)(2,1)}) %all-gather.3.cloned.1.call-update) | async-done | bytes 1572880 | tf_op jit(solution)/shard_map/all_gather | solution.py:63
  51.8 2.5 %multiply_reduce_fusion = (f32[6,256]{1,0:T(8,128)S(1)}, f32[6,256,1024]{2,1,0:T(8,128)S(1)}) fusion(bf16[256,6,128]{0,2,1:T(8,128)(2,1)S(1)} %bitcast.64, bf16[1024,6,128]{0,2,1:T(8,128)(2,1)} %bitcast.65), kind=kOutput, calls=%fused_computation.1 | convolution fusion | flops 405797376 | bytes 8263680 | tf_op jit(solution)/shard_map/qhd,khd->hqk/dot_general | solution.py:24
  54.4 0.0 copy-start
  54.4 0.1 fusion.19
  54.5 2.6 %copy-done = f32[6,256,1024]{2,1,0:T(8,128)} copy-done((f32[6,256,1024]{2,1,0:T(8,128)}, f32[6,256,1024]{2,1,0:T(8,128)S(1)}, u32[]{:S(2)}) %copy-start) | copy-done | bytes 6291480
  57.0 1.3 %fusion = f32[6,256]{1,0:T(8,128)S(1)} fusion(f32[6,256,1024]{2,1,0:T(8,128)S(1)} %get-tuple-element.15, f32[6,256]{1,0:T(8,128)S(1)} %get-tuple-element.11), kind=kLoop, calls=%fused_computation.2 | loop fusion | flops 4717056 | bytes 6303744 | tf_op jit(solution)/shard_map/reduce_sum | solution.py:33
  58.4 30.3 %all-gather.5.cloned.1.call-done = bf16[1024,768]{1,0:T(8,128)(2,1)} async-done(((bf16[256,768]{1,0:T(8,128)(2,1)}), bf16[1024,768]{1,0:T(8,128)(2,1)}) %all-gather.5.cloned.1.call-update) | async-done | bytes 1572880 | tf_op jit(solution)/shard_map/all_gather | solution.py:64
  88.7 1.7 %copy.23 = bf16[1024,768]{0,1:T(8,128)(2,1)S(1)} copy(bf16[1024,768]{1,0:T(8,128)(2,1)} %all-gather.5.cloned.1.call-done) | data formatting | bytes 3145728 | tf_op jit(solution)/shard_map/all_gather | solution.py:64
  90.4 0.0 copy-start.1
  90.4 4.3 %fusion.14 = f32[256,6,128]{0,2,1:T(8,128)S(1)} fusion(bf16[1024,6,128]{0,2,1:T(8,128)(2,1)S(1)} %bitcast.62, f32[6,256,1024]{2,1,0:T(8,128)} %copy-done, f32[6,256]{1,0:T(8,128)S(1)} %get-tuple-element.11, f32[256,6]{0,1:T(8,128)S(1)} %get-tuple-element.8, f32[256,6]{0,1:T(8,128)S(1)} %get-tuple-element.9), kind=kOutput, calls=%fused_computation.12 | convolution fusion | flops 407764992 | bytes 8669184 | tf_op jit(solution)/shard_map/hqk,khd->hqd/dot_general | solution.py:34
  94.7 0.4 multiply_reduce_fusion.1
  95.0 0.3 copy.30
  95.3 0.0 copy-done.1
  95.3 0.2 multiply_reduce_fusion.2
  95.5 6.4 %all-reduce = (f32[256]{0:T(256)S(1)}, f32[256]{0:T(256)S(1)}) all-reduce(f32[256]{0:T(256)S(1)} %get-tuple-element.16, f32[256]{0:T(256)S(1)} %multiply_reduce_fusion.2), channel_id=1, replica_groups=mesh['groups'=2,'seq'=4,'tensor'=4] {'tensor'}, use_global_device_ids=true, to_apply=%region_7.8 | all-reduce | flops 512 | bytes 4096 | tf_op jit(solution)/shard_map/psum | solution.py:76
  101.9 1.0 fusion.18
  (4 shorter events, 0.0 us)
Async XLA Ops:
  6.5 45.3 %all-gather.3.cloned.1.call-start = ((), (), s32[]{:S(2)}) async-start(), calls=%async_computation | async-start | bytes 1966080 | tf_op jit(solution)/shard_map/all_gather | solution.py:63
  8.5 80.2 %all-gather.5.cloned.1.call-start = ((), (), s32[]{:S(2)}) async-start(), calls=%async_computation.1 | async-start | bytes 1966080 | tf_op jit(solution)/shard_map/all_gather | solution.py:64
  54.4 2.7 %copy-start = (f32[6,256,1024]{2,1,0:T(8,128)}, f32[6,256,1024]{2,1,0:T(8,128)S(1)}, u32[]{:S(2)}) copy-start(f32[6,256,1024]{2,1,0:T(8,128)S(1)} %get-tuple-element.15) | copy-start | bytes 18874372
  90.4 4.9 %copy-start.1 = (bf16[256,768]{1,0:T(8,128)(2,1)S(1)}, bf16[256,768]{1,0:T(8,128)(2,1)}, u32[]{:S(2)}) copy-start(bf16[256,768]{1,0:T(8,128)(2,1)} %param.16) | copy-start | bytes 1179652
Sparse Core Ops, SparseCore 0:
  8.9 42.8 all-gather.2
  53.4 35.2 all-gather.4
where the time goes:
time: 110 us
  blocking collectives  39.2 us (36%)
  waiting for transfers between devices  36.7 us (33%)
  between operations  15.5 us (14%)
  local copies, waits for them, and re-layouts  7.62 us (7%)
  matrix products  7.35 us (7%)
  other arithmetic  3.31 us (3%)
    all_gather x1, waiting for transfers between devices, local(): lax.all_gather(values, 'seq', axis=0, tiled=True)  30.3 us
    all_gather x1, blocking collectives, local(): lax.all_gather(text_values, 'seq', axis=0, tiled=True)  17.1 us
    all_gather x1, blocking collectives, local(): lax.all_gather(text_keys, 'seq', axis=0, tiled=True)  15.7 us
    psum x1, blocking collectives, local(): lax.psum((jnp.sum(diff * cond, axis=1), jnp.sum(cond * cond, axis=1)), 't...  6.44 us
    all_gather x1, waiting for transfers between devices, local(): lax.all_gather(keys, 'seq', axis=0, tiled=True)  5.75 us
    unnamed x6, local copies, waits for them, and re-layouts  5.65 us
    dot_general x2, matrix products, attend(): jnp.einsum('hqk,khd->hqd', weights.astype(jnp.bfloat16), value_heads, pre...  4.62 us
    dot_general x2, matrix products, attend(): jnp.einsum('qhd,khd->hqk', query_heads, key_heads, preferred_element_type...  2.73 us
  transfers between devices with their start and end apart: 2, of which 2 were waited for; matrix products, arithmetic and copies ran while one was open for 5% of the time, Pallas kernels for 0%

commit v1 on v0

--- a/solution.py
+++ b/solution.py
@@ -1,11 +1,300 @@
+import functools
 import math
 
 import jax
 import jax.numpy as jnp
 from jax import lax
+from jax.experimental import pallas as pl
+from jax.experimental.pallas import tpu as pltpu
 from jax.sharding import PartitionSpec as P
 
 HEAD_DIM = 128
+SEQ = 4
+OWN_HEADS = 6
+MESH = pl.DeviceIdType.MESH
+K, V, TK, TV, Q = range(5)
+
+
+def kernel(
+    tensor_size,
+    q_hbm, k_hbm, v_hbm, tk_hbm, tv_hbm, len_ref, uncond_ref, flags_ref, num_ref, den_ref,
+    out_ref,
+    qs, ks, vs, cond, sums, stats,
+    own_sem, send_sem, recv_sem, back_send, back_recv, stat_send, stat_recv,
+):
+    rows = q_hbm.shape[0]
+    text_rows = tk_hbm.shape[0]
+    tokens = SEQ * rows
+    group = lax.axis_index("groups")
+    z = lax.axis_index("seq")
+    t = lax.axis_index("tensor")
+    core = lax.rem(t, 2)
+    half = z // 2
+    peers = (lax.rem(z + 2, SEQ), SEQ - 1 - z, z + 1 - 2 * lax.rem(z, 2))
+    has_extra = lax.rem(z, 2) == core
+
+    def at(seq, tensor):
+        return (group, seq, tensor)
+
+    sources = {K: k_hbm, V: v_hbm, TK: tk_hbm, TV: tv_hbm, Q: q_hbm}
+
+    def place(kind, slot, source):
+        if kind == Q:
+            return qs.at[slot, pl.ds(source * rows, rows), :]
+        big = ks if kind in (K, TK) else vs
+        if kind in (K, V):
+            return big.at[slot, pl.ds(source * rows, rows), :]
+        return big.at[slot, pl.ds(tokens + source * text_rows, text_rows), :]
+
+    def column(head):
+        return pl.ds(pl.multiple_of(head * HEAD_DIM, HEAD_DIM), HEAD_DIM)
+
+    def push(kind, slot, head, target):
+        return pltpu.make_async_remote_copy(
+            src_ref=sources[kind].at[:, column(head)],
+            dst_ref=place(kind, slot, z),
+            send_sem=send_sem.at[slot, kind, target],
+            recv_sem=recv_sem.at[slot, kind, z],
+            device_id=at(target, t),
+            device_id_type=MESH,
+        )
+
+    def arrival(kind, slot, source):
+        return pltpu.make_async_remote_copy(
+            src_ref=place(kind, slot, source),
+            dst_ref=place(kind, slot, source),
+            send_sem=send_sem.at[slot, kind, source],
+            recv_sem=recv_sem.at[slot, kind, source],
+            device_id=at(source, t),
+            device_id_type=MESH,
+        )
+
+    def keep(kind, slot, head):
+        return pltpu.make_async_copy(
+            sources[kind].at[:, column(head)], place(kind, slot, z), own_sem.at[slot, kind]
+        )
+
+    def give_back(slot, head, target):
+        return pltpu.make_async_remote_copy(
+            src_ref=qs.at[slot, pl.ds(target * rows, rows), :],
+            dst_ref=cond.at[head],
+            send_sem=back_send.at[slot, target],
+            recv_sem=back_recv.at[head],
+            device_id=at(target, t),
+            device_id_type=MESH,
+        )
+
+    kinds = (K, TK, V, TV, Q)
+    for kind in kinds:
+        keep(kind, 0, z).start()
+
+    @pl.when(has_extra)
+    def _():
+        for kind in kinds:
+            keep(kind, 1, SEQ + half).start()
+
+    barrier = pltpu.get_barrier_semaphore()
+    for peer in peers:
+        pl.semaphore_signal(barrier, inc=1, device_id=at(peer, t), device_id_type=MESH)
+    others = [lax.rem(t + step, tensor_size) for step in range(1, tensor_size)]
+    for other in others:
+        pl.semaphore_signal(barrier, inc=1, device_id=at(z, other), device_id_type=MESH)
+    pl.semaphore_wait(barrier, len(peers) + len(others))
+
+    far = 2 * (1 - half) + core
+    near = 2 * half + core
+    for kind in kinds:
+        push(kind, 1, SEQ + 1 - half, far).start()
+
+        @pl.when(jnp.logical_not(has_extra))
+        def _():
+            push(kind, 1, SEQ + half, near).start()
+
+    for kind in kinds:
+        for peer in peers:
+            push(kind, 0, peer, peer).start()
+
+    scale_log2 = math.log2(math.e) / math.sqrt(HEAD_DIM)
+    live = lax.broadcasted_iota(jnp.int32, (rows, SEQ * text_rows), 1) < len_ref[0]
+    contract = (((1,), (1,)), ((), ()))
+
+    def attend(slot, source, head):
+        query = qs[slot, pl.ds(source * rows, rows), :]
+        image = lax.dot_general(
+            query, ks[slot, pl.ds(0, tokens), :], contract, preferred_element_type=jnp.float32
+        )
+        text = lax.dot_general(
+            query,
+            ks[slot, pl.ds(tokens, SEQ * text_rows), :],
+            contract,
+            preferred_element_type=jnp.float32,
+        )
+        text = jnp.where(live, text * scale_log2, -1e30)
+        image = image * scale_log2
+        top = jnp.maximum(
+            jnp.max(image, axis=1, keepdims=True), jnp.max(text, axis=1, keepdims=True)
+        )
+        image = jnp.exp2(image - top)
+        text = jnp.exp2(text - top)
+        total = jnp.sum(image, axis=1, keepdims=True) + jnp.sum(text, axis=1, keepdims=True)
+        mixed = jnp.dot(
+            image.astype(jnp.bfloat16),
+            vs[slot, pl.ds(0, tokens), :],
+            preferred_element_type=jnp.float32,
+        ) + jnp.dot(
+            text.astype(jnp.bfloat16),
+            vs[slot, pl.ds(tokens, SEQ * text_rows), :],
+            preferred_element_type=jnp.float32,
+        )
+        return (mixed / total).astype(jnp.bfloat16)
+
+    def work(slot, head):
+        for kind in (K, TK, V, TV):
+            keep(kind, slot, head).wait()
+            for peer in peers:
+                arrival(kind, slot, peer).wait_recv()
+        keep(Q, slot, head).wait()
+        cond[head] = attend(slot, z, head)
+        for peer in peers:
+            arrival(Q, slot, peer).wait_recv()
+            result = attend(slot, peer, head)
+            qs[slot, pl.ds(peer * rows, rows), :] = result
+            give_back(slot, head, peer).start()
+
+    @pl.when(has_extra)
+    def _():
+        work(1, SEQ + half)
+
+    work(0, z)
+
+    def landed(head, source):
+        return pltpu.make_async_remote_copy(
+            src_ref=cond.at[head],
+            dst_ref=cond.at[head],
+            send_sem=back_send.at[0, source],
+            recv_sem=back_recv.at[head],
+            device_id=at(source, t),
+            device_id_type=MESH,
+        )
+
+    landed(SEQ + 1 - half, far).wait_recv()
+
+    @pl.when(jnp.logical_not(has_extra))
+    def _():
+        landed(SEQ + half, near).wait_recv()
+
+    for peer in peers:
+        landed(peer, peer).wait_recv()
+
+    inner = jnp.zeros((rows, HEAD_DIM), jnp.float32)
+    square = jnp.zeros((rows, HEAD_DIM), jnp.float32)
+    for head in range(OWN_HEADS):
+        mine = cond[head].astype(jnp.float32)
+        diff = mine - uncond_ref[:, head * HEAD_DIM : (head + 1) * HEAD_DIM].astype(jnp.float32)
+        inner += diff * mine
+        square += mine * mine
+    lane = lax.broadcasted_iota(jnp.int32, (rows, HEAD_DIM), 1)
+    pair = jnp.where(
+        lane == 0,
+        jnp.sum(inner, axis=1, keepdims=True),
+        jnp.sum(square, axis=1, keepdims=True),
+    )
+    sums[...] = pair.T[0:8, :]
+
+    def tell(step):
+        return pltpu.make_async_remote_copy(
+            src_ref=sums,
+            dst_ref=stats.at[step - 1],
+            send_sem=stat_send.at[step - 1],
+            recv_sem=stat_recv.at[step - 1],
+            device_id=at(z, lax.rem(t + step, tensor_size)),
+            device_id_type=MESH,
+        )
+
+    for step in range(1, tensor_size):
+        tell(step).start()
+    both = sums[...]
+    for step in range(1, tensor_size):
+        tell(step).wait_recv()
+        both = both + stats[step - 1]
+    width = tensor_size * OWN_HEADS * HEAD_DIM
+    coef = both[0:1, :] / width / (both[1:2, :] / width + 1e-6)
+    scale = num_ref[0].astype(jnp.float32) / den_ref[0].astype(jnp.float32)
+    alpha = jnp.where(flags_ref[...] > 0, scale - 1.0, 0.0)
+    line = lax.broadcasted_iota(jnp.int32, (HEAD_DIM, rows), 0)
+    columns = jnp.where(line == 0, coef, alpha).T
+    coef_column = columns[:, 0:1]
+    alpha_column = columns[:, 1:2]
+    for head in range(OWN_HEADS):
+        mine = cond[head].astype(jnp.float32)
+        span = slice(head * HEAD_DIM, (head + 1) * HEAD_DIM)
+        diff = mine - uncond_ref[:, span].astype(jnp.float32)
+        steered = mine + alpha_column * (diff - coef_column * mine)
+        out_ref[:, span] = steered.astype(jnp.bfloat16)
+
+    for step in range(1, tensor_size):
+        tell(step).wait_send()
+    for kind in kinds:
+        push(kind, 1, SEQ + 1 - half, far).wait_send()
+
+        @pl.when(jnp.logical_not(has_extra))
+        def _():
+            push(kind, 1, SEQ + half, near).wait_send()
+
+        for peer in peers:
+            push(kind, 0, peer, peer).wait_send()
+    for peer in peers:
+        give_back(0, z, peer).wait_send()
+
+    @pl.when(has_extra)
+    def _():
+        for peer in peers:
+            give_back(1, SEQ + half, peer).wait_send()
+
+
+def exchanged(
+    tensor_size,
+    queries, keys, values, text_keys, text_values, text_len, uncond, flags, guide_num, guide_den
+):
+    rows, width = queries.shape
+    text_rows = text_keys.shape[0]
+    joint = SEQ * (rows + text_rows)
+    hbm = pl.BlockSpec(memory_space=pl.ANY)
+    vmem = pl.BlockSpec(memory_space=pltpu.VMEM)
+    smem = pl.BlockSpec(memory_space=pltpu.SMEM)
+    dma = pltpu.SemaphoreType.DMA
+    return pl.pallas_call(
+        functools.partial(kernel, tensor_size),
+        out_shape=jax.ShapeDtypeStruct((rows, width), jnp.bfloat16),
+        in_specs=[hbm] * 5 + [smem, vmem, vmem, smem, smem],
+        out_specs=vmem,
+        scratch_shapes=[
+            pltpu.VMEM((2, SEQ * rows, HEAD_DIM), jnp.bfloat16),
+            pltpu.VMEM((2, joint, HEAD_DIM), jnp.bfloat16),
+            pltpu.VMEM((2, joint, HEAD_DIM), jnp.bfloat16),
+            pltpu.VMEM((OWN_HEADS, rows, HEAD_DIM), jnp.bfloat16),
+            pltpu.VMEM((8, rows), jnp.float32),
+            pltpu.VMEM((tensor_size - 1, 8, rows), jnp.float32),
+            dma((2, 5)),
+            dma((2, 5, SEQ)),
+            dma((2, 5, SEQ)),
+            dma((2, SEQ)),
+            dma((OWN_HEADS,)),
+            dma((tensor_size - 1,)),
+            dma((tensor_size - 1,)),
+        ],
+        compiler_params=pltpu.CompilerParams(
+            collective_id=0, has_side_effects=True, vmem_limit_bytes=40 * 1024 * 1024
+        ),
+        cost_estimate=pl.CostEstimate(
+            flops=4 * rows * joint * width,
+            bytes_accessed=10 * rows * width,
+            transcendentals=rows * joint * OWN_HEADS,
+        ),
+    )(
+        queries, keys, values, text_keys, text_values, text_len, uncond,
+        flags.reshape(1, rows), guide_num, guide_den,
+    )
 
 
 def local(
@@ -82,8 +371,20 @@
 
 
 def solution(mesh):
+    tensor_size = mesh.shape["tensor"]
+
+    def pick(queries, *rest):
+        fits = (
+            mesh.shape["seq"] == SEQ
+            and tensor_size % 2 == 0
+            and queries.shape[1] == OWN_HEADS * HEAD_DIM
+        )
+        if fits:
+            return exchanged(tensor_size, queries, *rest)
+        return local(queries, *rest)
+
     return jax.shard_map(
-        local,
+        pick,
         mesh=mesh,
         in_specs=(
             P(("groups", "seq"), "tensor"),

time: 110 us -> 54.2 us (0.49)
  Pallas kernels: 0 us -> 45 us
  blocking collectives: 39.2 us -> 0 us
  waiting for transfers between devices: 36.7 us -> 0 us
  between operations: 15.5 us -> 1.96 us
  matrix products: 7.35 us -> 0 us
  other arithmetic: 3.31 us -> 0 us
    pallas_call x0 -> x1, Pallas kernels: none -> 45 us  [exchanged(): pl.pallas_call(functools.partial(kernel, tensor_size), out_shape=jax.Shap...]
    all_gather x2 -> x0, waiting for transfers between devices: 36 us -> none  [the longest x1 30.3 us: local(): lax.all_gather(values, 'seq', axis=0, tiled=True)]
    all_gather x2 -> x0, blocking collectives: 32.8 us -> none  [the longest x1 17.1 us: local(): lax.all_gather(text_values, 'seq', axis=0, tiled=True)]
    dot_general x4 -> x0, matrix products: 7.35 us -> none  [the longest x2 4.62 us: attend(): jnp.einsum('hqk,khd->hqd', weights.astype(jnp.bfloat16), value_heads, pre...]
    psum x1 -> x0, blocking collectives: 6.44 us -> none  [local(): lax.psum((jnp.sum(diff * cond, axis=1), jnp.sum(cond * cond, axis=1)), 't...]
    all_gather x1 -> x0, local copies, waits for them, and re-layouts: 1.71 us -> none  [local(): lax.all_gather(values, 'seq', axis=0, tiled=True)]
    reduce_sum x3 -> x0, other arithmetic: 1.58 us -> none  [the longest x2 1.4 us: attend(): total = total * fade + jnp.sum(weights, axis=2)]
    unnamed x6 -> x15, local copies, waits for them, and re-layouts: 5.65 us -> 6.88 us
  transfers between devices with their start and end apart: 2 -> 0, of which waited for: 2 -> 0; matrix products, arithmetic and copies ran while one was open for 5% -> 0% of each run, Pallas kernels for 0% -> 0%
where the time goes in v1:
time: 54.2 us; the launch traced here: 53.8 us
  Pallas kernels  45 us (83%)
  local copies, waits for them, and re-layouts  6.88 us (13%)
  between operations  1.96 us (4%)
    pallas_call x1, Pallas kernels, exchanged(): pl.pallas_call(functools.partial(kernel, tensor_size), out_shape=jax.Shap...  45 us
    unnamed x15, local copies, waits for them, and re-layouts  6.88 us

profile of v1, /device:TPU:0, one launch (start us, length us, event | category | flops | bytes accessed | tf_op | source)
XLA Modules:
  0.0 53.8 jit_solution(15873995121142940710)
XLA Ops:
  1.9 0.0 copy-start.6
  2.0 0.7 %copy-done.6 = s32[256]{0:T(256)S(1)} copy-done((s32[256]{0:T(256)S(1)}, s32[256]{0:T(256)}, u32[]{:S(2)}) %copy-start.6) | copy-done | bytes 1048
  2.6 0.0 copy-start
  2.6 1.0 %copy-done = bf16[256,768]{1,0:T(8,128)(2,1)S(1)} copy-done((bf16[256,768]{1,0:T(8,128)(2,1)S(1)}, bf16[256,768]{1,0:T(8,128)(2,1)}, u32[]{:S(2)}) %copy-start) | copy-done | bytes 393240
  3.6 0.0 copy-start.1
  3.6 1.0 %copy-done.1 = bf16[256,768]{1,0:T(8,128)(2,1)S(1)} copy-done((bf16[256,768]{1,0:T(8,128)(2,1)S(1)}, bf16[256,768]{1,0:T(8,128)(2,1)}, u32[]{:S(2)}) %copy-start.1) | copy-done | bytes 393240
  4.6 0.0 copy-start.2
  4.6 1.0 %copy-done.2 = bf16[256,768]{1,0:T(8,128)(2,1)S(1)} copy-done((bf16[256,768]{1,0:T(8,128)(2,1)S(1)}, bf16[256,768]{1,0:T(8,128)(2,1)}, u32[]{:S(2)}) %copy-start.2) | copy-done | bytes 393240
  5.6 0.0 copy-start.3
  5.6 1.0 %copy-done.3 = bf16[256,768]{1,0:T(8,128)(2,1)S(1)} copy-done((bf16[256,768]{1,0:T(8,128)(2,1)S(1)}, bf16[256,768]{1,0:T(8,128)(2,1)}, u32[]{:S(2)}) %copy-start.3) | copy-done | bytes 393240
  6.6 0.0 copy-start.4
  6.6 0.7 %copy-done.4 = bf16[16,768]{1,0:T(8,128)(2,1)S(1)} copy-done((bf16[16,768]{1,0:T(8,128)(2,1)S(1)}, bf16[16,768]{1,0:T(8,128)(2,1)}, u32[]{:S(2)}) %copy-start.4) | copy-done | bytes 24600
  7.3 0.0 copy-start.5
  7.3 0.7 %copy-done.5 = bf16[16,768]{1,0:T(8,128)(2,1)S(1)} copy-done((bf16[16,768]{1,0:T(8,128)(2,1)S(1)}, bf16[16,768]{1,0:T(8,128)(2,1)}, u32[]{:S(2)}) %copy-start.5) | copy-done | bytes 24600
  8.1 45.0 %shard_map.100 = bf16[256,768]{1,0:T(8,128)(2,1)S(1)} custom-call(bf16[256,768]{1,0:T(8,128)(2,1)S(1)} %copy-done, bf16[256,768]{1,0:T(8,128)(2,1)S(1)} %copy-done.1, bf16[256,768]{1,0:T(8,128)(2,1)S(1)} %copy-done.2, bf16[16,768]{1,0:T(8,128)(2,1)S(1)} %copy-done.4, bf16[16,768]{1,0:T(8,128)(2,1)S(1)} %copy-done.5, s32[1]{0:T(128)S(6)} %copy.12.len_ref, ...), custom_call_target="tpu_custom_call" | custom-call | flops 855638016 | bytes 1966080 | tf_op jit(solution)/shard_map/pallas_call | solution.py:266
  53.1 0.7 %copy.15 = bf16[256,768]{1,0:T(8,128)(2,1)} copy(bf16[256,768]{1,0:T(8,128)(2,1)S(1)} %shard_map.100) | data formatting | bytes 786432
Async XLA Ops:
  1.9 0.7 %copy-start.6 = (s32[256]{0:T(256)S(1)}, s32[256]{0:T(256)}, u32[]{:S(2)}) copy-start(s32[256]{0:T(256)} %param.17) | copy-start | bytes 3076
  2.6 1.0 %copy-start = (bf16[256,768]{1,0:T(8,128)(2,1)S(1)}, bf16[256,768]{1,0:T(8,128)(2,1)}, u32[]{:S(2)}) copy-start(bf16[256,768]{1,0:T(8,128)(2,1)} %q_hbm.1) | copy-start | bytes 1179652
  3.6 1.0 %copy-start.1 = (bf16[256,768]{1,0:T(8,128)(2,1)S(1)}, bf16[256,768]{1,0:T(8,128)(2,1)}, u32[]{:S(2)}) copy-start(bf16[256,768]{1,0:T(8,128)(2,1)} %k_hbm.1) | copy-start | bytes 1179652
  4.6 1.0 %copy-start.2 = (bf16[256,768]{1,0:T(8,128)(2,1)S(1)}, bf16[256,768]{1,0:T(8,128)(2,1)}, u32[]{:S(2)}) copy-start(bf16[256,768]{1,0:T(8,128)(2,1)} %v_hbm.1) | copy-start | bytes 1179652
  5.6 1.0 %copy-start.3 = (bf16[256,768]{1,0:T(8,128)(2,1)S(1)}, bf16[256,768]{1,0:T(8,128)(2,1)}, u32[]{:S(2)}) copy-start(bf16[256,768]{1,0:T(8,128)(2,1)} %uncond_ref.1) | copy-start | bytes 1179652
  6.6 0.7 %copy-start.4 = (bf16[16,768]{1,0:T(8,128)(2,1)S(1)}, bf16[16,768]{1,0:T(8,128)(2,1)}, u32[]{:S(2)}) copy-start(bf16[16,768]{1,0:T(8,128)(2,1)} %tk_hbm.1) | copy-start | bytes 73732
  7.3 0.7 %copy-start.5 = (bf16[16,768]{1,0:T(8,128)(2,1)S(1)}, bf16[16,768]{1,0:T(8,128)(2,1)}, u32[]{:S(2)}) copy-start(bf16[16,768]{1,0:T(8,128)(2,1)} %tv_hbm.1) | copy-start | bytes 73732

commit v2 on v1

--- a/solution.py
+++ b/solution.py
@@ -17,10 +17,10 @@
 
 def kernel(
     tensor_size,
-    q_hbm, k_hbm, v_hbm, tk_hbm, tv_hbm, len_ref, uncond_ref, flags_ref, num_ref, den_ref,
+    q_hbm, k_hbm, v_hbm, tk_hbm, tv_hbm, len_ref, uncond_hbm, flags_hbm, num_ref, den_ref,
     out_ref,
-    qs, ks, vs, cond, sums, stats,
-    own_sem, send_sem, recv_sem, back_send, back_recv, stat_send, stat_recv,
+    qs, ks, vs, cond, sums, stats, uncond_ref, flags_ref,
+    side_sem, own_sem, send_sem, recv_sem, back_send, back_recv, stat_send, stat_recv,
 ):
     rows = q_hbm.shape[0]
     text_rows = tk_hbm.shape[0]
@@ -84,14 +84,16 @@
             device_id_type=MESH,
         )
 
+    side = [
+        pltpu.make_async_copy(source, target, side_sem.at[index])
+        for index, (source, target) in enumerate(
+            (
+                (flags_hbm, flags_ref),
+                (uncond_hbm, uncond_ref),
+            )
+        )
+    ]
     kinds = (K, TK, V, TV, Q)
-    for kind in kinds:
-        keep(kind, 0, z).start()
-
-    @pl.when(has_extra)
-    def _():
-        for kind in kinds:
-            keep(kind, 1, SEQ + half).start()
 
     barrier = pltpu.get_barrier_semaphore()
     for peer in peers:
@@ -113,6 +115,17 @@
     for kind in kinds:
         for peer in peers:
             push(kind, 0, peer, peer).start()
+
+    for copy in side:
+        copy.start()
+
+    @pl.when(has_extra)
+    def _():
+        for kind in kinds:
+            keep(kind, 1, SEQ + half).start()
+
+    for kind in kinds:
+        keep(kind, 0, z).start()
 
     scale_log2 = math.log2(math.e) / math.sqrt(HEAD_DIM)
     live = lax.broadcasted_iota(jnp.int32, (rows, SEQ * text_rows), 1) < len_ref[0]
@@ -177,6 +190,8 @@
             device_id_type=MESH,
         )
 
+    for copy in side:
+        copy.wait()
     landed(SEQ + 1 - half, far).wait_recv()
 
     @pl.when(jnp.logical_not(has_extra))
@@ -266,7 +281,7 @@
     return pl.pallas_call(
         functools.partial(kernel, tensor_size),
         out_shape=jax.ShapeDtypeStruct((rows, width), jnp.bfloat16),
-        in_specs=[hbm] * 5 + [smem, vmem, vmem, smem, smem],
+        in_specs=[hbm] * 5 + [smem, hbm, hbm, smem, smem],
         out_specs=vmem,
         scratch_shapes=[
             pltpu.VMEM((2, SEQ * rows, HEAD_DIM), jnp.bfloat16),
@@ -275,6 +290,9 @@
             pltpu.VMEM((OWN_HEADS, rows, HEAD_DIM), jnp.bfloat16),
             pltpu.VMEM((8, rows), jnp.float32),
             pltpu.VMEM((tensor_size - 1, 8, rows), jnp.float32),
+            pltpu.VMEM((rows, width), jnp.bfloat16),
+            pltpu.VMEM((1, rows), jnp.int32),
+            dma((2,)),
             dma((2, 5)),
             dma((2, 5, SEQ)),
             dma((2, 5, SEQ)),
@@ -284,7 +302,7 @@
             dma((tensor_size - 1,)),
         ],
         compiler_params=pltpu.CompilerParams(
-            collective_id=0, has_side_effects=True, vmem_limit_bytes=40 * 1024 * 1024
+            collective_id=0, has_side_effects=True, vmem_limit_bytes=60 * 1024 * 1024
         ),
         cost_estimate=pl.CostEstimate(
             flops=4 * rows * joint * width,

time: 54.2 us -> 49.8 us (0.919)
  local copies, waits for them, and re-layouts: 6.88 us -> 1.77 us
  Pallas kernels: 45 us -> 45.9 us
    unnamed x15 -> x1, local copies, waits for them, and re-layouts: 6.88 us -> 1.77 us
    pallas_call x1, Pallas kernels: 45 us -> 45.9 us  [exchanged(): pl.pallas_call(functools.partial(kernel, tensor_size), out_shape=jax.Shap...]
where the time goes in v2:
time: 49.8 us; the launch traced here: 49.6 us
  Pallas kernels  45.9 us (92%)
  between operations  1.95 us (4%)
  local copies, waits for them, and re-layouts  1.77 us (4%)
    pallas_call x1, Pallas kernels, exchanged(): pl.pallas_call(functools.partial(kernel, tensor_size), out_shape=jax.Shap...  45.9 us
    unnamed x1, local copies, waits for them, and re-layouts  1.77 us

profile of v2, /device:TPU:0, one launch (start us, length us, event | category | flops | bytes accessed | tf_op | source)
XLA Modules:
  0.0 49.6 jit_solution(14943253149144836338)
XLA Ops:
  1.9 45.9 %shard_map.100 = bf16[256,768]{1,0:T(8,128)(2,1)} custom-call(bf16[256,768]{1,0:T(8,128)(2,1)} %q_hbm.1, bf16[256,768]{1,0:T(8,128)(2,1)} %k_hbm.1, bf16[256,768]{1,0:T(8,128)(2,1)} %v_hbm.1, bf16[16,768]{1,0:T(8,128)(2,1)} %tk_hbm.1, bf16[16,768]{1,0:T(8,128)(2,1)} %tv_hbm.1, s32[1]{0:T(128)S(6)} %copy.12.len_ref, bf16[256,768]{1,0:T(8,128)(2,1)} %uncond_hbm.1, ...), custom_call_target="tpu_custom_call" | custom-call | flops 855638016 | bytes 1966080 | tf_op jit(solution)/shard_map/pallas_call | solution.py:281
  47.9 1.8 %copy.15 = bf16[256,768]{1,0:T(8,128)(2,1)} copy(bf16[256,768]{1,0:T(8,128)(2,1)} %shard_map.100) | data formatting | bytes 786432

commit v3 on v2

--- a/solution.py
+++ b/solution.py
@@ -166,13 +166,13 @@
             keep(kind, slot, head).wait()
             for peer in peers:
                 arrival(kind, slot, peer).wait_recv()
-        keep(Q, slot, head).wait()
-        cond[head] = attend(slot, z, head)
         for peer in peers:
             arrival(Q, slot, peer).wait_recv()
             result = attend(slot, peer, head)
             qs[slot, pl.ds(peer * rows, rows), :] = result
             give_back(slot, head, peer).start()
+        keep(Q, slot, head).wait()
+        cond[head] = attend(slot, z, head)
 
     @pl.when(has_extra)
     def _():
@@ -192,22 +192,26 @@
 
     for copy in side:
         copy.wait()
+    def add_up(head, so_far):
+        inner, square = so_far
+        mine = cond[head].astype(jnp.float32)
+        other = uncond_ref[:, column(head)].astype(jnp.float32)
+        return inner + (mine - other) * mine, square + mine * mine
+
+    zero = jnp.zeros((rows, HEAD_DIM), jnp.float32)
+    so_far = add_up(z, (zero, zero))
     landed(SEQ + 1 - half, far).wait_recv()
+    so_far = add_up(SEQ + 1 - half, so_far)
 
     @pl.when(jnp.logical_not(has_extra))
     def _():
         landed(SEQ + half, near).wait_recv()
 
+    so_far = add_up(SEQ + half, so_far)
     for peer in peers:
         landed(peer, peer).wait_recv()
-
-    inner = jnp.zeros((rows, HEAD_DIM), jnp.float32)
-    square = jnp.zeros((rows, HEAD_DIM), jnp.float32)
-    for head in range(OWN_HEADS):
-        mine = cond[head].astype(jnp.float32)
-        diff = mine - uncond_ref[:, head * HEAD_DIM : (head + 1) * HEAD_DIM].astype(jnp.float32)
-        inner += diff * mine
-        square += mine * mine
+        so_far = add_up(peer, so_far)
+    inner, square = so_far
     lane = lax.broadcasted_iota(jnp.int32, (rows, HEAD_DIM), 1)
     pair = jnp.where(
         lane == 0,
@@ -267,6 +271,10 @@
             give_back(1, SEQ + half, peer).wait_send()
 
 
+def pinned(*arrays):
+    return [pltpu.with_memory_space_constraint(array, pltpu.HBM) for array in arrays]
+
+
 def exchanged(
     tensor_size,
     queries, keys, values, text_keys, text_values, text_len, uncond, flags, guide_num, guide_den
@@ -274,7 +282,7 @@
     rows, width = queries.shape
     text_rows = text_keys.shape[0]
     joint = SEQ * (rows + text_rows)
-    hbm = pl.BlockSpec(memory_space=pl.ANY)
+    hbm = pl.BlockSpec(memory_space=pltpu.HBM)
     vmem = pl.BlockSpec(memory_space=pltpu.VMEM)
     smem = pl.BlockSpec(memory_space=pltpu.SMEM)
     dma = pltpu.SemaphoreType.DMA
@@ -302,7 +310,7 @@
             dma((tensor_size - 1,)),
         ],
         compiler_params=pltpu.CompilerParams(
-            collective_id=0, has_side_effects=True, vmem_limit_bytes=60 * 1024 * 1024
+            collective_id=0, has_side_effects=True, vmem_limit_bytes=48 * 1024 * 1024
         ),
         cost_estimate=pl.CostEstimate(
             flops=4 * rows * joint * width,
@@ -310,8 +318,8 @@
             transcendentals=rows * joint * OWN_HEADS,
         ),
     )(
-        queries, keys, values, text_keys, text_values, text_len, uncond,
-        flags.reshape(1, rows), guide_num, guide_den,
+        *pinned(queries, keys, values, text_keys, text_values), text_len,
+        *pinned(uncond, flags.reshape(1, rows)), guide_num, guide_den,
     )
 
 

time: 49.8 us -> 48 us (0.964)
  local copies, waits for them, and re-layouts: 1.77 us -> 0.75 us
  Pallas kernels: 45.9 us -> 45.1 us
    unnamed x1, local copies, waits for them, and re-layouts: 1.77 us -> 0.75 us
    pallas_call x1, Pallas kernels: 45.9 us -> 45.1 us  [exchanged(): pl.pallas_call(functools.partial(kernel, tensor_size), out_shape=jax.Shap...]
where the time goes in v3:
time: 48 us; the launch traced here: 47.8 us
  Pallas kernels  45.1 us (94%)
  between operations  1.95 us (4%)
  local copies, waits for them, and re-layouts  0.75 us (2%)
    pallas_call x1, Pallas kernels, exchanged(): pl.pallas_call(functools.partial(kernel, tensor_size), out_shape=jax.Shap...  45.1 us

profile of v3, /device:TPU:0, one launch (start us, length us, event | category | flops | bytes accessed | tf_op | source)
XLA Modules:
  0.0 47.8 jit_solution(13804795312876661347)
XLA Ops:
  1.9 45.1 %shard_map.100 = bf16[256,768]{1,0:T(8,128)(2,1)S(1)} custom-call(bf16[256,768]{1,0:T(8,128)(2,1)} %q_hbm.1, bf16[256,768]{1,0:T(8,128)(2,1)} %k_hbm.1, bf16[256,768]{1,0:T(8,128)(2,1)} %v_hbm.1, bf16[16,768]{1,0:T(8,128)(2,1)} %tk_hbm.1, bf16[16,768]{1,0:T(8,128)(2,1)} %tv_hbm.1, s32[1]{0:T(128)S(6)} %copy.12.len_ref, bf16[256,768]{1,0:T(8,128)(2,1)} %uncond_hbm.1, ...), custom_call_target="tpu_custom_call" | custom-call | flops 855638016 | bytes 1966080 | tf_op jit(solution)/shard_map/pallas_call | solution.py:289
  47.1 0.7 %copy.15 = bf16[256,768]{1,0:T(8,128)(2,1)} copy(bf16[256,768]{1,0:T(8,128)(2,1)S(1)} %shard_map.100) | data formatting | bytes 786432
